TPU v7x, 32 devices: a whole 2x2x4 slice. The times are simulated.
32 devices in a mesh: rows: 16 (over z, y, x), cols: 2 (over core).
Axes of the slice: x: 2, y: 2, z: 4, core: 2. Of those that a mesh axis runs over, the one named last changes fastest.
Arguments:
- momentum_codes: int32 [2, 8192, 8192], P(None, 'rows', 'cols'), may hold values from 0 to 255
- block_amax_scales: float32 [2, 8192, 4], P(None, 'rows'), may hold values from 0.05 to 1
- code_table: float32 [256], replicated, may hold values from -1 to 1
- gradient: bfloat16 [2, 8192, 8192], P(None, 'rows', 'cols'), may hold values from -4 to 4
- weight: bfloat16 [2, 8192, 8192], P(None, 'rows', 'cols'), may hold values from -6 to 6
- right_basis: bfloat16 [2, 8192, 256], P(None, 'cols'), may hold values from -0.0625 to 0.0625
Outputs:
- new_momentum: bfloat16 [2, 8192, 8192], P(None, 'rows', 'cols')
- fresh_block_scales: float32 [2, 8192, 4], P(None, 'rows')
- new_basis: bfloat16 [2, 8192, 256], P(None, 'cols')
- new_weight: bfloat16 [2, 8192, 8192], P(None, 'rows', 'cols')
All inputs are finite; a program needn't handle non-finite values.
Results may differ from a plain program's by a relative error of at most 0.005.
Values sent between devices are 32-bit elements; how exact they have to be, the bound alone decides.
A program may use at most 192 MiB of HBM per device.

v0:
```python
import math

import jax
import jax.numpy as jnp
from jax import lax
from jax.sharding import PartitionSpec as P

D = 8192
RANK = 256
BLOCK = 2048


epsilon = 1e-06
momentum_decay = 0.95
step_size = 0.5


def triangular_solved_rows(cholesky_lower, row_block):
    return jax.scipy.linalg.solve_triangular(cholesky_lower, row_block.T, lower=True).T


def decode(momentum_codes, code_table):
    upper_part = code_table.astype(jnp.bfloat16)
    remainder = code_table - upper_part.astype(jnp.float32)
    middle_part = remainder.astype(jnp.bfloat16)
    lower_part = (remainder - middle_part.astype(jnp.float32)).astype(jnp.bfloat16)
    table_parts = jnp.stack([upper_part, middle_part, lower_part])
    matrices, row_count, col_count = momentum_codes.shape
    total_rows = matrices * row_count
    group_rows = math.gcd(total_rows, 16)
    grouped = momentum_codes.reshape(total_rows // group_rows, group_rows * col_count)
    level_ids = jnp.arange(code_table.shape[0], dtype=jnp.int32)[:, None]

    def decode_group(flat_codes):
        one_hot = (flat_codes[None, :] == level_ids).astype(jnp.bfloat16)
        return jnp.sum(jnp.dot(table_parts, one_hot, preferred_element_type=jnp.float32), axis=0)

    decoded = lax.map(decode_group, grouped)
    return decoded.reshape(matrices, row_count, col_count)


def per_device(momentum_codes, block_amax_scales, code_table, gradient, weight, right_basis):
    peak_magnitude = lax.Precision.HIGHEST
    col_count = momentum_codes.shape[2]
    block_count = D // BLOCK
    col_start = lax.axis_index("cols") * col_count
    block_ids = (col_start + jnp.arange(col_count, dtype=jnp.int32)) // BLOCK
    block_mask = block_ids[None, :] == jnp.arange(block_count, dtype=jnp.int32)[:, None]
    value_range = block_mask.astype(jnp.float32)
    values = decode(momentum_codes, code_table)
    scale_columns = jnp.einsum(
        "kol,lq->koq", block_amax_scales, value_range, precision=peak_magnitude
    )
    buffer = values * scale_columns + gradient.astype(jnp.float32)
    partial_power = jnp.einsum(
        "mrn,mnk->mrk", buffer, right_basis.astype(jnp.float32), precision=peak_magnitude
    )
    power_rows = lax.psum(partial_power, "cols")
    gram_piece = jnp.einsum("mrk,mrl->mkl", power_rows, power_rows, precision=peak_magnitude)
    basis_gram_product = lax.psum(gram_piece, "rows")
    cholesky_lower = jnp.linalg.cholesky(basis_gram_product)
    ortho_rows = jax.vmap(triangular_solved_rows)(cholesky_lower, power_rows)
    partial_back = jnp.einsum("mrn,mrk->mnk", buffer, ortho_rows, precision=peak_magnitude)
    back_rows = lax.psum(partial_back, "rows")
    square_sums = lax.psum(jnp.sum(back_rows * back_rows, axis=1), "cols")
    basis_full = back_rows * lax.rsqrt(square_sums + epsilon)[:, None, :]
    residual = buffer - (1.0 - momentum_decay) * jnp.einsum(
        "mrk,mnk->mrn", ortho_rows, back_rows, precision=peak_magnitude
    )
    magnitude = jnp.abs(residual)
    partial_max = jnp.max(jnp.where(block_mask[None, None], magnitude[:, :, None, :], 0.0), axis=3)
    fresh_block_scales = lax.pmax(partial_max, "cols")
    fresh_scale_columns = jnp.einsum(
        "kol,lq->koq", fresh_block_scales, value_range, precision=peak_magnitude
    )
    new_momentum = (residual / (fresh_scale_columns + epsilon)).astype(jnp.bfloat16)
    update = jnp.einsum("mrk,mnk->mrn", ortho_rows, basis_full, precision=peak_magnitude) * (
        D / math.sqrt(RANK)
    )
    new_weight = (weight.astype(jnp.float32) - step_size * update).astype(jnp.bfloat16)
    return (new_momentum, fresh_block_scales, basis_full.astype(jnp.bfloat16), new_weight)


def solution(mesh):
    placed = (
        P(None, "rows", "cols"),
        P(None, "rows", None),
        P(),
        P(None, "rows", "cols"),
        P(None, "rows", "cols"),
        P(None, "cols", None),
    )
    return jax.shard_map(
        per_device,
        mesh=mesh,
        in_specs=placed,
        out_specs=(
            P(None, "rows", "cols"),
            P(None, "rows", None),
            P(None, "cols", None),
            P(None, "rows", "cols"),
        ),
        check_vma=False,
    )
```

profile of v0, /device:TPU:0, one launch (start us, length us, event | category | flops | bytes accessed | tf_op | source)
XLA Modules:
  0.0 1961.7 jit_solution(15552691063978356198)
XLA Ops:
  7.3 14.5 reshape.79
  21.9 1183.0 %while.13 = (s32[]{:T(128)}, f32[64,65536]{1,0:T(8,128)}, s32[64,65536]{1,0:T(8,128)}, bf16[3,256]{1,0:T(4,128)(2,1)S(1)}, s32[]{:T(128)}, /*index=5*/s32[]{:T(128)}) while((s32[]{:T(128)}, f32[64,65536]{1,0:T(8,128)}, s32[64,65536]{1,0:T(8,128)}, bf16[3,256]{1,0:T(4,128)(2,1)S(1)}, s32[]{:T(128)}, /*index=5*/s32[]{:T(128)}) %tuple.49), condition=%wide.region_2.3_spmd.clone, body=%wide.region_0.2_spmd.clone.sunk | while | flops 117571584 | bytes 1574485 | solution.py:38
  23.7 10.7 fusion.49
  42.1 10.7 fusion.49
  60.6 10.7 fusion.49
  79.1 10.7 fusion.49
  97.6 10.7 fusion.49
  116.1 10.7 fusion.49
  134.6 10.7 fusion.49
  153.1 10.7 fusion.49
  171.5 10.7 fusion.49
  190.0 10.7 fusion.49
  208.5 10.7 fusion.49
  227.0 10.7 fusion.49
  245.5 10.7 fusion.49
  264.0 10.7 fusion.49
  282.4 10.7 fusion.49
  300.9 10.7 fusion.49
  319.4 10.7 fusion.49
  337.9 10.7 fusion.49
  356.4 10.7 fusion.49
  374.8 10.7 fusion.49
  393.3 10.7 fusion.49
  411.8 10.7 fusion.49
  430.3 10.7 fusion.49
  448.7 10.7 fusion.49
  467.2 10.7 fusion.49
  485.7 10.7 fusion.49
  504.2 10.7 fusion.49
  522.7 10.7 fusion.49
  541.2 10.7 fusion.49
  559.6 10.7 fusion.49
  578.1 10.7 fusion.49
  596.6 10.7 fusion.49
  615.1 10.7 fusion.49
  633.6 10.7 fusion.49
  652.1 10.7 fusion.49
  670.5 10.7 fusion.49
  744.5 10.7 fusion.49
  799.9 10.7 fusion.49
  855.4 10.7 fusion.49
  910.9 10.7 fusion.49
  984.9 10.7 fusion.49
  1058.8 10.7 fusion.49
  1151.2 10.7 fusion.49
  1204.9 14.5 reshape.80
  1219.4 17.5 copy.47
  1236.9 11.9 copy.48
  1248.8 15.8 fusion.5
  1264.6 18.0 fusion.29
  1282.7 22.4 %all-reduce.5.cloned.1.call-done = f32[2,512,256]{2,1,0:T(8,128)} async-done(((f32[2,512,256]{2,1,0:T(8,128)}), f32[2,512,256]{2,1,0:T(8,128)}) %all-reduce.5.cloned.1.call-update) | async-done | bytes 1048592 | tf_op jit(solution)/shard_map/psum | solution.py:58
  1309.5 111.7 %all-reduce.7.cloned.1.call-done = f32[2,256,256]{1,2,0:T(8,128)} async-done(((f32[2,256,256]{1,2,0:T(8,128)}), f32[2,256,256]{1,2,0:T(8,128)}) %all-reduce.7.cloned.1.call-update) | async-done | bytes 524304 | tf_op jit(solution)/shard_map/psum | solution.py:60
  1423.5 23.9 %custom-call.17 = f32[2,128,128]{2,1,0:T(8,128)S(1)} custom-call(f32[2,128,128]{2,1,0:T(8,128)S(1)} %cholesky.122), custom_call_target="Cholesky" | custom-call | tf_op jit(solution)/shard_map/jit(cholesky)/cholesky | solution.py:61
  1447.4 19.7 %custom-call.18 = f32[2,1,128,128]{2,3,1,0:T(8,128)S(1)} custom-call(f32[2,1,128,128]{3,2,1,0:T(8,128)S(1)} %select_bitcast_fusion), custom_call_target="InvertDiagBlocksLowerTriangular" | custom-call | tf_op jit(solution)/shard_map/jit(cholesky)/cholesky | solution.py:61
  1467.8 23.5 %custom-call.19 = f32[2,128,128]{2,1,0:T(8,128)S(1)} custom-call(f32[2,128,128]{2,1,0:T(8,128)S(1)} %convolution_subtract_fusion.1), custom_call_target="Cholesky" | custom-call | tf_op jit(solution)/shard_map/jit(cholesky)/cholesky | solution.py:61
  1495.7 39.5 %custom-call.20 = f32[2,2,128,128]{2,3,1,0:T(8,128)S(1)} custom-call(f32[2,2,128,128]{3,2,1,0:T(8,128)S(1)} %bitcast.67), custom_call_target="InvertDiagBlocksLowerTriangular" | custom-call | tf_op jit(solution)/shard_map/vmap(jit(_solve_triangular))/triangular_solve | solution.py:19
  1539.6 18.8 fusion.8
  1558.5 255.4 %all-reduce.9.cloned.1.call-done = f32[2,4096,256]{2,1,0:T(8,128)} async-done(((f32[2,4096,256]{2,1,0:T(8,128)}), f32[2,4096,256]{2,1,0:T(8,128)}) %all-reduce.9.cloned.1.call-update) | async-done | bytes 8388624 | tf_op jit(solution)/shard_map/psum | solution.py:64
  1813.9 27.2 %fusion.28 = (f32[2,512,4096]{1,2,0:T(8,128)}, f32[2,512,4096]{1,2,0:T(8,128)}) fusion(f32[2,512,4096]{1,2,0:T(8,128)} %fusion.5, f32[2,4096,256]{2,1,0:T(8,128)} %all-reduce.9.cloned.1.call-done, f32[2,128,512]{2,1,0:T(8,128)S(1)} %fusion.13, f32[2,128,512]{2,1,0:T(8,128)S(1)} %fusion.9), kind=kOutput, calls=%fused_computation.67 | convolution fusion | flops 12897746944 | bytes 59768832 | tf_op jit(solution)/shard_map/mrk,mnk->mrn/dot_general | solution.py:67
  1841.1 17.5 copy.63
  1858.6 11.3 select_reduce_fusion
  1873.3 13.5 divide_convert_fusion
  1886.8 11.9 copy.66
  1911.3 43.4 %subtract_convert_fusion = bf16[2,512,4096]{2,1,0:T(8,128)(2,1)} fusion(bf16[2,512,4096]{2,1,0:T(8,128)(2,1)} %param.12, f32[2,4096,256]{2,1,0:T(8,128)} %all-reduce.9.cloned.1.call-done, f32[2,256]{1,0:T(2,128)S(1)} %add_rsqrt_fusion, f32[2,128,512]{2,1,0:T(8,128)S(1)} %fusion.13, f32[2,128,512]{2,1,0:T(8,128)S(1)} %fusion.9), kind=kOutput, calls=%fused_computation.11 | convolution fusion | flops 12904038400 | bytes 26216448 | tf_op jit(solution)/shard_map/mrk,mnk->mrn/dot_general | solution.py:77
  (206 shorter events, 760.0 us)
Async XLA Ops:
  7.2 1241.7 %copy-start = (f32[2,512,4]{1,2,0:T(4,128)S(1)}, f32[2,512,4]{1,2,0:T(4,128)}, u32[]{:S(2)}) copy-start(f32[2,512,4]{1,2,0:T(4,128)} %param.9) | copy-start | bytes 49156
  7.2 1297.9 %all-reduce.5.cloned.1.call-start = ((), (), s32[]{:S(2)}) async-start(), calls=%async_computation | async-start | bytes 2097152 | tf_op jit(solution)/shard_map/psum | solution.py:58
  7.2 14.6 copy-start.4
  1248.8 15.8 copy-start.2
  1282.6 138.5 %all-reduce.7.cloned.1.call-start = ((), (), s32[]{:S(2)}) async-start(), calls=%async_computation.1 | async-start | bytes 1048576 | tf_op jit(solution)/shard_map/psum | solution.py:60
  1309.3 504.6 %all-reduce.9.cloned.1.call-start = ((), (), s32[]{:S(2)}) async-start(), calls=%async_computation.2 | async-start | bytes 16777216 | tf_op jit(solution)/shard_map/psum | solution.py:64
  1873.3 13.5 copy-start.3
  1905.2 49.5 %copy-start.1 = (f32[2,512,4]{1,2,0:T(4,128)S(1)}, f32[2,512,4]{1,2,0:T(4,128)}, u32[]{:S(2)}) copy-start(f32[2,512,4]{1,2,0:T(4,128)} %param.9) | copy-start | bytes 49156
Sparse Core Ops, SparseCore 0:
  1282.7 22.2 all-reduce.4
  1311.6 109.4 all-reduce.6
  1558.5 255.2 all-reduce.8
where the time goes:
time: 1980 us; the launch traced here: 1960 us
  matrix products  828 us (42%)
  local copies, waits for them, and re-layouts  593 us (30%)
  waiting for transfers between devices  390 us (20%)
  other arithmetic  129 us (7%)
    dot_general x64, matrix products, decode_group(): jnp.dot(table_parts, one_hot, preferred_element_type=jnp.float32)  682 us
    dynamic_update_slice x64, local copies, waits for them, and re-layouts, decode(): decoded = lax.map(decode_group, grouped)  386 us
    psum x1, waiting for transfers between devices, per_device(): back_rows = lax.psum(partial_back, 'rows')  255 us
    dynamic_slice x64, local copies, waits for them, and re-layouts, decode(): decoded = lax.map(decode_group, grouped)  113 us
    psum x1, waiting for transfers between devices, per_device(): basis_gram_product = lax.psum(gram_piece, 'rows')  112 us
    another operation x9, other arithmetic, per_device(): cholesky_lower = jnp.linalg.cholesky(basis_gram_product)  67.2 us
    dot_general x1, matrix products, per_device(): jnp.einsum('mrk,mnk->mrn', ortho_rows, basis_full, precision=peak_magnitude)  43.4 us
    another operation x4, other arithmetic, triangular_solved_rows(): jax.scipy.linalg.solve_triangular(cholesky_lower, row_block.T, lower=True)  39.7 us
  transfers between devices with their start and end apart: 3, of which 3 were waited for; matrix products, arithmetic and copies ran while one was open for 0% of the time, Pallas kernels for 0%

commit v1 on v0

v1 whole, which is shorter than its diff:
```python
import functools
import math

import jax
import jax.numpy as jnp
from jax import lax
from jax.experimental import pallas as pl
from jax.experimental.pallas import tpu as pltpu
from jax.sharding import PartitionSpec as P

BLOCK = 2048
LANES = 128
epsilon = 1e-06
momentum_decay = 0.95
step_size = 0.5
HIGHEST = lax.Precision.HIGHEST
VMEM_LIMIT = 56 * 1024 * 1024


def params(**more):
    return pltpu.CompilerParams(vmem_limit_bytes=VMEM_LIMIT, **more)


def decode_kernel(span, codes_ref, scale_ref, table_ref, grad_ref, basis_ref, hi_ref, power_ref, lo_ref):
    rows, cols = hi_ref.shape[1:]
    sub = min(rows, 64)
    parts = table_ref.shape[0]

    def row_step(i, carry):
        at = pl.ds(pl.multiple_of(i * sub, sub), sub)
        tables = [jnp.broadcast_to(table_ref[p : p + 1, :], (sub, LANES)) for p in range(parts)]
        for c in range(cols // LANES):
            cut = slice(c * LANES, (c + 1) * LANES)
            codes = codes_ref[0, at, cut]
            low = codes % LANES if parts == 1 else lax.bitwise_and(codes, LANES - 1)
            value = jnp.take_along_axis(tables[0], low, axis=1)
            for p in range(1, parts):
                value = jnp.where(codes >= p * LANES, jnp.take_along_axis(tables[p], low, axis=1), value)
            block = (c * LANES) // span
            scale = scale_ref[0, at, block : block + 1]
            whole = value * scale + grad_ref[0, at, cut].astype(jnp.float32)
            hi = whole.astype(jnp.bfloat16)
            hi_ref[0, at, cut] = hi
            lo_ref[at, cut] = (whole - hi.astype(jnp.float32)).astype(jnp.bfloat16)
        return carry

    lax.fori_loop(0, rows // sub, row_step, 0)
    basis = basis_ref[0]
    power_ref[0] = jnp.dot(hi_ref[0], basis, preferred_element_type=jnp.float32) + jnp.dot(
        lo_ref[...], basis, preferred_element_type=jnp.float32
    )


def decode_power(codes, scales, table, gradient, basis):
    mats, rows, cols = codes.shape
    rank = basis.shape[2]
    tile = min(rows, 256)
    blocks = scales.shape[2]
    span = cols // blocks
    halves = table.reshape(-1, LANES)
    return pl.pallas_call(
        functools.partial(decode_kernel, span),
        grid=(mats, rows // tile),
        in_specs=[
            pl.BlockSpec((1, tile, cols), lambda m, i: (m, i, 0)),
            pl.BlockSpec((1, tile, blocks), lambda m, i: (m, i, 0)),
            pl.BlockSpec(halves.shape, lambda m, i: (0, 0)),
            pl.BlockSpec((1, tile, cols), lambda m, i: (m, i, 0)),
            pl.BlockSpec((1, cols, rank), lambda m, i: (m, 0, 0)),
        ],
        out_specs=[
            pl.BlockSpec((1, tile, cols), lambda m, i: (m, i, 0)),
            pl.BlockSpec((1, tile, rank), lambda m, i: (m, i, 0)),
        ],
        out_shape=[
            jax.ShapeDtypeStruct((mats, rows, cols), jnp.bfloat16),
            jax.ShapeDtypeStruct((mats, rows, rank), jnp.float32),
        ],
        scratch_shapes=[pltpu.VMEM((tile, cols), jnp.bfloat16)],
        compiler_params=params(),
        cost_estimate=pl.CostEstimate(flops=4 * mats * rows * cols * rank, bytes_accessed=8 * mats * rows * cols, transcendentals=0),
    )(codes, scales, halves, gradient, basis)


def gram_of(rows_block):
    return lax.dot_general(
        rows_block, rows_block, (((0,), (0,)), ((), ())), precision=HIGHEST, preferred_element_type=jnp.float32
    )


def gram_kernel(power_ref, gram_ref):
    gram_ref[0] = gram_of(power_ref[0])


def gram_local(power):
    mats, rows, rank = power.shape
    return pl.pallas_call(
        gram_kernel,
        grid=(mats,),
        in_specs=[pl.BlockSpec((1, rows, rank), lambda m: (m, 0, 0))],
        out_specs=pl.BlockSpec((1, rank, rank), lambda m: (m, 0, 0)),
        out_shape=jax.ShapeDtypeStruct((mats, rank, rank), jnp.float32),
        compiler_params=params(),
    )(power)


def cross_kernel(power_ref, hi_ref, cross_ref, turned_ref):
    @pl.when(pl.program_id(1) == 0)
    def _():
        turned_ref[...] = power_ref[0].T.astype(jnp.bfloat16)

    cross_ref[0] = jnp.dot(turned_ref[...], hi_ref[0], preferred_element_type=jnp.float32)


def cross_local(power, hi):
    mats, rows, cols = hi.shape
    rank = power.shape[2]
    tile = min(cols, 1024)
    return pl.pallas_call(
        cross_kernel,
        grid=(mats, cols // tile),
        in_specs=[
            pl.BlockSpec((1, rows, rank), lambda m, j: (m, 0, 0)),
            pl.BlockSpec((1, rows, tile), lambda m, j: (m, 0, j)),
        ],
        out_specs=pl.BlockSpec((1, rank, tile), lambda m, j: (m, 0, j)),
        out_shape=jax.ShapeDtypeStruct((mats, rank, cols), jnp.float32),
        scratch_shapes=[pltpu.VMEM((rank, rows), jnp.bfloat16)],
        compiler_params=params(),
    )(power, hi)


def back_kernel(inverse_ref, cross_ref, back_ref, square_ref):
    back = jnp.dot(inverse_ref[0], cross_ref[0], precision=HIGHEST, preferred_element_type=jnp.float32)
    back_ref[0] = back
    squares = jnp.sum(back * back, axis=1, keepdims=True)
    first = pl.program_id(1) == 0

    @pl.when(first)
    def _():
        square_ref[0] = squares

    @pl.when(jnp.logical_not(first))
    def _():
        square_ref[0] += squares


def back_local(inverse, cross):
    mats, rank, cols = cross.shape
    tile = min(cols, 1024)
    return pl.pallas_call(
        back_kernel,
        grid=(mats, cols // tile),
        in_specs=[
            pl.BlockSpec((1, rank, rank), lambda m, j: (m, 0, 0)),
            pl.BlockSpec((1, rank, tile), lambda m, j: (m, 0, j)),
        ],
        out_specs=[
            pl.BlockSpec((1, rank, tile), lambda m, j: (m, 0, j)),
            pl.BlockSpec((1, rank, 1), lambda m, j: (m, 0, 0)),
        ],
        out_shape=[
            jax.ShapeDtypeStruct((mats, rank, cols), jnp.float32),
            jax.ShapeDtypeStruct((mats, rank, 1), jnp.float32),
        ],
        compiler_params=params(),
    )(inverse, cross)


def final_kernel(
    whole_blocks, factor, power_ref, inverse_ref, norm_ref, back_ref, part_ref, hi_ref, weight_ref,
    momentum_ref, peak_ref, basis_ref, weight_out_ref, back16_ref,
):
    @pl.when(pl.program_id(1) == 0)
    def _():
        back16_ref[...] = back_ref[0].astype(jnp.bfloat16)

    tile, cols = hi_ref.shape[1:]
    ortho = lax.dot_general(
        power_ref[0], inverse_ref[0], (((1,), (1,)), ((), ())), precision=HIGHEST, preferred_element_type=jnp.float32
    )
    inv_norm = lax.rsqrt(norm_ref[0] + epsilon)
    left = jnp.concatenate([ortho * (1.0 - momentum_decay), ortho * inv_norm * factor], axis=0).astype(jnp.bfloat16)
    span = min(cols, BLOCK)
    for b in range(cols // span):
        at = slice(b * span, (b + 1) * span)
        both = jnp.dot(left, back16_ref[:, at], preferred_element_type=jnp.float32)
        residual = hi_ref[0, :, at].astype(jnp.float32) - both[:tile]
        peak = jnp.max(jnp.abs(residual), axis=1, keepdims=True)
        peak_ref[0, :, b : b + 1] = peak
        if whole_blocks:
            momentum_ref[0, :, at] = (residual * (1.0 / (peak + epsilon))).astype(momentum_ref.dtype)
        else:
            momentum_ref[0, :, at] = residual.astype(momentum_ref.dtype)
        weight_out_ref[0, :, at] = (weight_ref[0, :, at].astype(jnp.float32) - both[tile:]).astype(jnp.bfloat16)
    basis_ref[0] = (part_ref[0].T * inv_norm).astype(jnp.bfloat16)


def final_local(power, inverse, norms, back, hi, weight, factor):
    mats, rows, cols = hi.shape
    rank = power.shape[2]
    tile = min(rows, 128)
    steps = rows // tile
    part = cols // steps
    span = min(cols, BLOCK)
    whole_blocks = cols % BLOCK == 0
    held = jnp.bfloat16 if whole_blocks else jnp.float32
    return pl.pallas_call(
        functools.partial(final_kernel, whole_blocks, factor),
        grid=(mats, steps),
        in_specs=[
            pl.BlockSpec((1, tile, rank), lambda m, i: (m, i, 0)),
            pl.BlockSpec((1, rank, rank), lambda m, i: (m, 0, 0)),
            pl.BlockSpec((1, 1, rank), lambda m, i: (m, 0, 0)),
            pl.BlockSpec((1, rank, cols), lambda m, i: (m, 0, 0)),
            pl.BlockSpec((1, rank, part), lambda m, i: (m, 0, i)),
            pl.BlockSpec((1, tile, cols), lambda m, i: (m, i, 0)),
            pl.BlockSpec((1, tile, cols), lambda m, i: (m, i, 0)),
        ],
        out_specs=[
            pl.BlockSpec((1, tile, cols), lambda m, i: (m, i, 0)),
            pl.BlockSpec((1, tile, cols // span), lambda m, i: (m, i, 0)),
            pl.BlockSpec((1, part, rank), lambda m, i: (m, i, 0)),
            pl.BlockSpec((1, tile, cols), lambda m, i: (m, i, 0)),
        ],
        out_shape=[
            jax.ShapeDtypeStruct((mats, rows, cols), held),
            jax.ShapeDtypeStruct((mats, rows, cols // span), jnp.float32),
            jax.ShapeDtypeStruct((mats, cols, rank), jnp.bfloat16),
            jax.ShapeDtypeStruct((mats, rows, cols), jnp.bfloat16),
        ],
        scratch_shapes=[pltpu.VMEM((rank, cols), jnp.bfloat16)],
        compiler_params=params(),
    )(power, inverse, norms, back, back, hi, weight)


def spread_peaks(peaks, col_start, cols, blocks):
    starts = (col_start + jnp.arange(peaks.shape[2], dtype=jnp.int32) * min(cols, BLOCK)) // BLOCK
    hit = starts[:, None] == jnp.arange(blocks, dtype=jnp.int32)[None, :]
    return lax.pmax(jnp.max(jnp.where(hit[None, None], peaks[..., None], 0.0), axis=2), "cols")


def per_device(codes, scales, table, gradient, weight, basis):
    mats, rows, cols = codes.shape
    blocks = scales.shape[2]
    total_cols = blocks * BLOCK
    rank = basis.shape[2]
    col_start = lax.axis_index("cols") * cols
    span = min(cols, BLOCK)
    local_blocks = cols // span
    own_scales = lax.dynamic_slice_in_dim(scales, col_start // BLOCK, local_blocks, axis=2)
    hi, partial_power = decode_power(codes, own_scales, table, gradient, basis)
    power = lax.psum(partial_power, "cols")
    gram = lax.psum(gram_local(power), "rows")
    cross = lax.psum(cross_local(power, hi), "rows")
    lower = jnp.linalg.cholesky(gram)
    eye = jnp.broadcast_to(jnp.eye(rank, dtype=jnp.float32), gram.shape)
    inverse = lax.linalg.triangular_solve(lower, eye, left_side=True, lower=True)
    back, squares = back_local(inverse, cross)
    norms = lax.psum(squares, "cols").reshape(mats, 1, rank)
    factor = step_size * total_cols / math.sqrt(rank)
    momentum, peaks, new_basis, new_weight = final_local(power, inverse, norms, back, hi, weight, factor)
    fresh = spread_peaks(peaks, col_start, cols, blocks)
    if cols % BLOCK != 0:
        own = lax.dynamic_slice_in_dim(fresh, col_start // BLOCK, local_blocks, axis=2)
        columns = jnp.broadcast_to(own[..., None], own.shape + (span,)).reshape(mats, rows, cols)
        momentum = (momentum / (columns + epsilon)).astype(jnp.bfloat16)
    return momentum, fresh, new_basis, new_weight


def solution(mesh):
    placed = (
        P(None, "rows", "cols"),
        P(None, "rows", None),
        P(),
        P(None, "rows", "cols"),
        P(None, "rows", "cols"),
        P(None, "cols", None),
    )
    return jax.shard_map(
        per_device,
        mesh=mesh,
        in_specs=placed,
        out_specs=(
            P(None, "rows", "cols"),
            P(None, "rows", None),
            P(None, "cols", None),
            P(None, "rows", "cols"),
        ),
        check_vma=False,
    )
```

time: 1980 us -> 529 us (0.27)
  matrix products: 828 us -> 1.86 us
  local copies, waits for them, and re-layouts: 593 us -> 10.3 us
  waiting for transfers between devices: 390 us -> 293 us
  Pallas kernels: 0 us -> 92 us
    dot_general x71 -> x0, matrix products: 823 us -> none  [the longest x64 682 us: decode_group(): jnp.dot(table_parts, one_hot, preferred_element_type=jnp.float32)]
    dynamic_update_slice x64 -> x0, local copies, waits for them, and re-layouts: 386 us -> none  [decode(): decoded = lax.map(decode_group, grouped)]
    dynamic_slice x64 -> x1, local copies, waits for them, and re-layouts: 113 us -> 0.01 us  [per_device(): lax.dynamic_slice_in_dim(scales, col_start // BLOCK, local_blocks, axis=2)]
    psum x3 -> x2, waiting for transfers between devices: 389 us -> 293 us  [the longest x1 271 us: per_device(): gram = lax.psum(gram_local(power), 'rows')]
    pallas_call x0 -> x5, Pallas kernels: none -> 92 us  [the longest x1 39.3 us: decode_power(): pl.pallas_call(functools.partial(decode_kernel, span), grid=(mats, rows /...]
    reshape x3 -> x1, local copies, waits for them, and re-layouts: 46.5 us -> 0.01 us  [per_device(): norms = lax.psum(squares, 'cols').reshape(mats, 1, rank)]
    unnamed x12 -> x5, local copies, waits for them, and re-layouts: 23.9 us -> 1.68 us
  transfers between devices with their start and end apart: 3 -> 2, of which waited for: 3 -> 2; matrix products, arithmetic and copies ran while one was open for 0% -> 0% of each run, Pallas kernels for 0% -> 0%
where the time goes in v1:
time: 529 us
  waiting for transfers between devices  293 us (55%)
  other arithmetic  110 us (21%)
  Pallas kernels  92 us (17%)
  between operations  14.3 us (3%)
  local copies, waits for them, and re-layouts  10.3 us (2%)
  blocking collectives  7 us (1%)
    psum x1, waiting for transfers between devices, per_device(): gram = lax.psum(gram_local(power), 'rows')  271 us
    another operation x9, other arithmetic, per_device(): lower = jnp.linalg.cholesky(gram)  66.8 us
    another operation x5, other arithmetic, per_device(): lax.linalg.triangular_solve(lower, eye, left_side=True, lower=True)  40.3 us
    pallas_call x1, Pallas kernels, decode_power(): pl.pallas_call(functools.partial(decode_kernel, span), grid=(mats, rows /...  39.3 us
    pallas_call x1, Pallas kernels, final_local(): pl.pallas_call(functools.partial(final_kernel, whole_blocks, factor), gri...  25.3 us
    psum x1, waiting for transfers between devices, per_device(): power = lax.psum(partial_power, 'cols')  22.4 us
    pallas_call x1, Pallas kernels, back_local(): pl.pallas_call(back_kernel, grid=(mats, cols // tile), in_specs=[pl.Block...  13.1 us
    pallas_call x1, Pallas kernels, cross_local(): pl.pallas_call(cross_kernel, grid=(mats, cols // tile), in_specs=[pl.Bloc...  11 us
  transfers between devices with their start and end apart: 2, of which 2 were waited for; matrix products, arithmetic and copies ran while one was open for 0% of the time, Pallas kernels for 0%

profile of v1, /device:TPU:0, one launch (start us, length us, event | category | flops | bytes accessed | tf_op | source)
XLA Modules:
  0.0 528.5 jit_solution(12991557594302775183)
XLA Ops:
  7.2 0.0 copy-start
  7.2 0.0 all-reduce.5.cloned.1.call-start
  7.2 0.6 copy-done
  7.9 1.0 copy.42.scale_ref
  8.9 39.3 %shard_map.93 = (bf16[2,512,4096]{2,1,0:T(8,128)(2,1)}, f32[2,512,256]{2,1,0:T(8,128)}) custom-call(s32[2,512,4096]{2,1,0:T(8,128)} %codes_ref.1, f32[2,512,2]{2,1,0:T(8,128)} %copy.42.scale_ref, f32[2,128]{1,0:T(2,128)} %bitcast.37, bf16[2,512,4096]{2,1,0:T(8,128)(2,1)} %grad_ref.1, bf16[2,4096,256]{2,1,0:T(8,128)(2,1)} %basis_ref.1), custom_call_target="tpu_custom_call" | custom-call | flops 4294967296 | bytes 33554432 | tf_op jit(solution)/shard_map/pallas_call | solution.py:61
  48.3 0.0 all-reduce.5.cloned.1.call-update
  48.3 0.0 all-reduce.7.cloned.1.call-start
  48.4 22.4 %all-reduce.5.cloned.1.call-done.power_ref = f32[2,512,256]{2,1,0:T(8,128)} async-done(((f32[2,512,256]{2,1,0:T(8,128)}), f32[2,512,256]{2,1,0:T(8,128)}) %all-reduce.5.cloned.1.call-update) | async-done | bytes 1048592 | tf_op jit(solution)/shard_map/psum | solution.py:253
  70.8 3.2 shard_map.94
  74.0 2.0 copy.28
  76.0 11.0 %shard_map.95 = f32[2,256,4096]{2,1,0:T(8,128)} custom-call(f32[2,512,256]{2,1,0:T(8,128)} %all-reduce.5.cloned.1.call-done.power_ref, bf16[2,512,4096]{2,1,0:T(8,128)(2,1)} %get-tuple-element.13.hi_ref), custom_call_target="tpu_custom_call" | custom-call | tf_op jit(solution)/shard_map/pallas_call | solution.py:119
  87.0 0.0 all-reduce.7.cloned.1.call-update
  87.2 0.1 iota_compare_fusion.4
  87.3 270.9 %all-reduce.7.cloned.1.call-done = (f32[2,256,256]{1,2,0:T(8,128)}, f32[2,256,4096]{2,1,0:T(8,128)}) async-done(((f32[2,256,256]{1,2,0:T(8,128)}, f32[2,256,4096]{2,1,0:T(8,128)}), (f32[2,256,256]{1,2,0:T(8,128)}, f32[2,256,4096]{2,1,0:T(8,128)})) %all-reduce.7.cloned.1.call-update) | async-done | bytes 8912912 | tf_op jit(solution)/shard_map/psum | solution.py:254
  358.1 1.2 copy.29
  359.4 1.1 fusion
  360.5 23.5 %custom-call.16 = f32[2,128,128]{2,1,0:T(8,128)S(1)} custom-call(f32[2,128,128]{2,1,0:T(8,128)S(1)} %cholesky.122), custom_call_target="Cholesky" | custom-call | tf_op jit(solution)/shard_map/jit(cholesky)/cholesky | solution.py:256
  384.0 19.7 %custom-call.17 = f32[2,1,128,128]{2,3,1,0:T(8,128)S(1)} custom-call(f32[2,1,128,128]{3,2,1,0:T(8,128)S(1)} %select_bitcast_fusion), custom_call_target="InvertDiagBlocksLowerTriangular" | custom-call | tf_op jit(solution)/shard_map/jit(cholesky)/cholesky | solution.py:256
  403.7 0.3 constant_dynamic-update-slice_fusion.1
  404.0 0.4 convolution_subtract_fusion.1
  404.4 23.5 %custom-call.18 = f32[2,128,128]{2,1,0:T(8,128)S(1)} custom-call(f32[2,128,128]{2,1,0:T(8,128)S(1)} %convolution_subtract_fusion.1), custom_call_target="Cholesky" | custom-call | tf_op jit(solution)/shard_map/jit(cholesky)/cholesky | solution.py:256
  427.9 0.2 compare_reduce_fusion
  428.1 0.1 select_select_fusion
  428.2 0.1 triangular_solve.66
  428.3 4.2 while.1
  428.5 0.6 fusion.16
  429.0 1.4 bitcast_dynamic-update-slice_fusion.2
  430.5 0.6 fusion.16
  431.1 1.4 bitcast_dynamic-update-slice_fusion.2
  432.5 39.3 %custom-call.19 = f32[2,2,128,128]{2,3,1,0:T(8,128)S(1)} custom-call(f32[2,2,128,128]{3,2,1,0:T(8,128)S(1)} %bitcast.38), custom_call_target="InvertDiagBlocksLowerTriangular" | custom-call | tf_op jit(solution)/shard_map/triangular_solve | solution.py:258
  471.8 0.4 fusion.4
  472.2 0.4 convolution_subtract_fusion
  472.6 0.4 fusion.3
  473.0 0.8 pad_maximum_fusion.inverse_ref
  473.9 13.1 %shard_map.96 = (f32[2,256,4096]{2,1,0:T(8,128)}, f32[2,256,1]{2,1,0:T(8,128)}) custom-call(f32[2,256,256]{2,1,0:T(8,128)} %pad_maximum_fusion.inverse_ref, f32[2,256,4096]{2,1,0:T(8,128)} %get-tuple-element.39.cross_ref), custom_call_target="tpu_custom_call" | custom-call | tf_op jit(solution)/shard_map/pallas_call | solution.py:151
  487.0 1.1 reduce.12
  488.1 3.0 psum.31.norm_ref
  491.1 0.0 copy-start.1
  491.1 25.3 %shard_map.97 = (bf16[2,512,4096]{2,1,0:T(8,128)(2,1)}, f32[2,512,2]{2,1,0:T(8,128)}, bf16[2,4096,256]{2,1,0:T(8,128)(2,1)}, bf16[2,512,4096]{2,1,0:T(8,128)(2,1)}) custom-call(f32[2,512,256]{2,1,0:T(8,128)} %all-reduce.5.cloned.1.call-done.power_ref, f32[2,256,256]{2,1,0:T(8,128)} %pad_maximum_fusion.inverse_ref, f32[2,1,256]{2,1,0:T(1,128)} %psum.31.norm_ref, ...), custom_call_target="tpu_custom_call" | custom-call | tf_op jit(solution)/shard_map/pallas_call | solution.py:208
  516.4 1.2 copy.36
  517.6 0.1 select_reduce_fusion.2
  517.7 4.0 pmax.7
  521.7 0.0 copy-done.1
  (17 shorter events, 0.3 us)
Async XLA Ops:
  7.2 0.7 copy-start
  7.2 63.6 %all-reduce.5.cloned.1.call-start = ((), (), s32[]{:S(2)}) async-start(), calls=%async_computation | async-start | bytes 2097152 | tf_op jit(solution)/shard_map/psum | solution.py:253
  48.3 309.8 %all-reduce.7.cloned.1.call-start = ((), (), s32[]{:S(2)}) async-start(), calls=%async_computation.1 | async-start | bytes 17825792 | tf_op jit(solution)/shard_map/psum | solution.py:254
  491.1 30.6 %copy-start.1 = (f32[2,512,4]{1,2,0:T(4,128)S(1)}, f32[2,512,4]{1,2,0:T(4,128)}, u32[]{:S(2)}) copy-start(f32[2,512,4]{1,2,0:T(4,128)} %param.7) | copy-start | bytes 49156
Sparse Core Ops, SparseCore 0:
  48.4 22.2 all-reduce.4
  87.2 270.9 all-reduce.6

commit v2 on v1

--- a/solution.py
+++ b/solution.py
@@ -240,6 +240,104 @@
     return lax.pmax(jnp.max(jnp.where(hit[None, None], peaks[..., None], 0.0), axis=2), "cols")
 
 
+def factor_kernel(gram_ref, out_ref, left_ref, right_ref):
+    mats, rank = gram_ref.shape[:2]
+    side = left_ref.shape[1]
+    rows = lax.broadcasted_iota(jnp.int32, (side, side), 0)
+    lanes = lax.broadcasted_iota(jnp.int32, (side, side), 1)
+    full = lambda a, b: lax.dot_general(
+        a, b, (((1,), (0,)), ((), ())), precision=HIGHEST, preferred_element_type=jnp.float32
+    )
+    trail = [gram_ref[m] for m in range(mats)]
+    wide_rows = lax.broadcasted_iota(jnp.int32, (rank, rank), 0)
+    wide_lanes = lax.broadcasted_iota(jnp.int32, (rank, rank), 1)
+    grown = [(wide_rows == wide_lanes).astype(jnp.float32) for _ in range(mats)]
+    for b in range(rank // side):
+        at = slice(b * side, (b + 1) * side)
+        for m in range(mats):
+            left_ref[m] = trail[m][at, at]
+            right_ref[m] = (rows == lanes).astype(jnp.float32)
+
+        def step(j, carry):
+            for m in range(mats):
+                left = left_ref[m]
+                column = jnp.sum(jnp.where(lanes == j, left, 0.0), axis=1, keepdims=True)
+                row = left_ref[m, pl.ds(j, 1), :]
+                pivot = jnp.sum(jnp.where(lanes[:1] == j, row, 0.0), axis=1, keepdims=True)
+                ratio = jnp.where(rows[:, :1] > j, column / pivot, 0.0)
+                other = right_ref[m, pl.ds(j, 1), :]
+                left_ref[m] = left - ratio * row
+                right_ref[m] = right_ref[m] - ratio * other
+            return carry
+
+        lax.fori_loop(0, side, step, 0)
+        for m in range(mats):
+            pivots = jnp.sum(jnp.where(rows == lanes, left_ref[m], 0.0), axis=1, keepdims=True)
+            block = right_ref[m] * lax.rsqrt(pivots)
+            upper = full(block, trail[m][at, :])
+            top = full(block, grown[m][at, :])
+            out_ref[m, at, :] = top
+            if (b + 1) * side < rank:
+                lower = jnp.where(wide_rows[:, :side] >= (b + 1) * side, upper.T, 0.0)
+                trail[m] = trail[m] - full(lower, upper)
+                grown[m] = grown[m] - full(lower, top)
+
+
+def inverse_factor(gram):
+    mats, rank = gram.shape[:2]
+    side = min(rank, LANES)
+    return pl.pallas_call(
+        factor_kernel,
+        out_shape=jax.ShapeDtypeStruct(gram.shape, jnp.float32),
+        scratch_shapes=[pltpu.VMEM((mats, side, side), jnp.float32), pltpu.VMEM((mats, side, side), jnp.float32)],
+        compiler_params=params(),
+        cost_estimate=pl.CostEstimate(flops=1500 * mats * rank**3, bytes_accessed=8 * mats * rank * rank, transcendentals=0),
+    )(gram)
+
+
+def swap(value, axis, size, bit):
+    return lax.ppermute(value, axis, [(i, i ^ (1 << bit)) for i in range(size)])
+
+
+def doubled_sum(value, axis):
+    size = lax.axis_size(axis)
+    if size & (size - 1):
+        return lax.psum(value, axis)
+    for bit in range(size.bit_length() - 1):
+        value = value + swap(value, axis, size, bit)
+    return value
+
+
+def halved_sum(value, axis, early):
+    size = lax.axis_size(axis)
+    height = value.shape[1]
+    if size & (size - 1) or height % size or size < 4:
+        return lax.psum(value, axis), early
+    cols = value.shape[2]
+    first = cols * 3 // 8
+    bits = list(range(size.bit_length() - 1))
+    turn = len(bits) // 2
+    orders = [bits, [bits[1], bits[0]] + bits[2:], bits[turn:] + bits[:turn]]
+    parts = [value[:, :, :first], value[:, :, first : 2 * first], value[:, :, 2 * first :]]
+    place = lax.axis_index(axis)
+    for step in range(len(bits)):
+        for p, order in enumerate(orders):
+            side = (place >> order[step]) & 1
+            half = parts[p].shape[1] // 2
+            away = lax.dynamic_slice_in_dim(parts[p], (1 - side) * half, half, axis=1)
+            kept = lax.dynamic_slice_in_dim(parts[p], side * half, half, axis=1)
+            parts[p] = kept + swap(away, axis, size, order[step])
+    *parts, early = lax.optimization_barrier((*parts, early))
+    for step in reversed(range(len(bits))):
+        for p, order in enumerate(orders):
+            upper = ((place >> order[step]) & 1) == 1
+            other = swap(parts[p], axis, size, order[step])
+            parts[p] = jnp.concatenate(
+                [jnp.where(upper, other, parts[p]), jnp.where(upper, parts[p], other)], axis=1
+            )
+    return jnp.concatenate(parts, axis=2), early
+
+
 def per_device(codes, scales, table, gradient, weight, basis):
     mats, rows, cols = codes.shape
     blocks = scales.shape[2]
@@ -250,12 +348,10 @@
     local_blocks = cols // span
     own_scales = lax.dynamic_slice_in_dim(scales, col_start // BLOCK, local_blocks, axis=2)
     hi, partial_power = decode_power(codes, own_scales, table, gradient, basis)
-    power = lax.psum(partial_power, "cols")
-    gram = lax.psum(gram_local(power), "rows")
-    cross = lax.psum(cross_local(power, hi), "rows")
-    lower = jnp.linalg.cholesky(gram)
-    eye = jnp.broadcast_to(jnp.eye(rank, dtype=jnp.float32), gram.shape)
-    inverse = lax.linalg.triangular_solve(lower, eye, left_side=True, lower=True)
+    power = doubled_sum(partial_power, "cols")
+    gram = doubled_sum(gram_local(power), "rows")
+    cross, gram = halved_sum(cross_local(power, hi), "rows", gram)
+    inverse = inverse_factor(gram)
     back, squares = back_local(inverse, cross)
     norms = lax.psum(squares, "cols").reshape(mats, 1, rank)
     factor = step_size * total_cols / math.sqrt(rank)

time: 529 us -> 362 us (0.68)
  waiting for transfers between devices: 293 us -> 128 us
  other arithmetic: 110 us -> 25.8 us
  Pallas kernels: 92 us -> 149 us
  starting transfers between devices: 0.08 us -> 36 us
  between operations: 14.3 us -> 1.07 us
    psum x2 -> x0, waiting for transfers between devices: 293 us -> none  [the longest x1 271 us: per_device(): gram = lax.psum(gram_local(power), 'rows')]
    ppermute x0 -> x29, waiting for transfers between devices: none -> 128 us  [swap(): return lax.ppermute(value, axis, [(i, i ^ 1 << bit) for i in range(size)])]
    another operation x14 -> x0, other arithmetic: 107 us -> none  [the longest x9 66.8 us: per_device(): lower = jnp.linalg.cholesky(gram)]
    pallas_call x0 -> x1, Pallas kernels: none -> 56.9 us  [inverse_factor(): pl.pallas_call(factor_kernel, out_shape=jax.ShapeDtypeStruct(gram.shape,...]
    ppermute x0 -> x29, starting transfers between devices: none -> 36 us  [swap(): return lax.ppermute(value, axis, [(i, i ^ 1 << bit) for i in range(size)])]
    add x0 -> x17, other arithmetic: none -> 14 us  [the longest x5 7.4 us: doubled_sum(): value = value + swap(value, axis, size, bit)]
    select_n x0 -> x11, other arithmetic: none -> 5.38 us  [halved_sum(): jnp.where(upper, other, parts[p])]
  transfers between devices with their start and end apart: 2 -> 29, of which waited for: 2 -> 18; matrix products, arithmetic and copies ran while one was open for 0% -> 7% of each run, Pallas kernels for 0% -> 19%
where the time goes in v2:
time: 362 us; the launch traced here: 361 us
  Pallas kernels  149 us (41%)
  waiting for transfers between devices  128 us (35%)
  starting transfers between devices  36 us (10%)
  other arithmetic  25.8 us (7%)
  local copies, waits for them, and re-layouts  13.7 us (4%)
  blocking collectives  7 us (2%)
    ppermute x29, waiting for transfers between devices, swap(): return lax.ppermute(value, axis, [(i, i ^ 1 << bit) for i in range(size)])  128 us
    pallas_call x1, Pallas kernels, inverse_factor(): pl.pallas_call(factor_kernel, out_shape=jax.ShapeDtypeStruct(gram.shape,...  56.9 us
    pallas_call x1, Pallas kernels, decode_power(): pl.pallas_call(functools.partial(decode_kernel, span), grid=(mats, rows /...  39.4 us
    ppermute x29, starting transfers between devices, swap(): return lax.ppermute(value, axis, [(i, i ^ 1 << bit) for i in range(size)])  36 us
    pallas_call x1, Pallas kernels, final_local(): pl.pallas_call(functools.partial(final_kernel, whole_blocks, factor), gri...  25.3 us
    pallas_call x1, Pallas kernels, back_local(): pl.pallas_call(back_kernel, grid=(mats, cols // tile), in_specs=[pl.Block...  13.1 us
    pallas_call x1, Pallas kernels, cross_local(): pl.pallas_call(cross_kernel, grid=(mats, cols // tile), in_specs=[pl.Bloc...  11 us
    add x5, other arithmetic, doubled_sum(): value = value + swap(value, axis, size, bit)  7.4 us
  transfers between devices with their start and end apart: 29, of which 18 were waited for; matrix products, arithmetic and copies ran while one was open for 7% of the time, Pallas kernels for 19%

profile of v2, /device:TPU:0, one launch (start us, length us, event | category | flops | bytes accessed | tf_op | source)
XLA Modules:
  0.0 360.9 jit_solution(10757294464178655287)
XLA Ops:
  1.4 1.0 copy.16.scale_ref
  2.4 39.4 %shard_map.93 = (bf16[2,512,4096]{2,1,0:T(8,128)(2,1)}, f32[2,512,256]{2,1,0:T(8,128)}) custom-call(s32[2,512,4096]{2,1,0:T(8,128)} %codes_ref.1, f32[2,512,2]{2,1,0:T(8,128)} %copy.16.scale_ref, f32[2,128]{1,0:T(2,128)} %bitcast.1, bf16[2,512,4096]{2,1,0:T(8,128)(2,1)} %grad_ref.1, bf16[2,4096,256]{2,1,0:T(8,128)(2,1)} %basis_ref.1), custom_call_target="tpu_custom_call" | custom-call | flops 4294967296 | bytes 33554432 | tf_op jit(solution)/shard_map/pallas_call | solution.py:61
  42.2 2.5 collective-permute-done
  44.7 2.3 add.137.power_ref
  47.0 3.2 shard_map.95
  50.3 2.9 collective-permute-start.13
  53.1 11.0 %shard_map.94 = f32[2,256,4096]{2,1,0:T(8,128)} custom-call(f32[2,512,256]{2,1,0:T(8,128)} %add.137.power_ref, bf16[2,512,4096]{2,1,0:T(8,128)(2,1)} %get-tuple-element.17.hi_ref), custom_call_target="tpu_custom_call" | custom-call | tf_op jit(solution)/shard_map/pallas_call | solution.py:119
  64.1 1.7 slice.14
  65.9 1.1 constant_dynamic-slice_fusion.3
  67.0 1.6 collective-permute-start.9
  68.6 0.9 add.170
  69.5 1.5 collective-permute-start.14
  71.0 3.3 fusion
  74.3 1.4 constant_dynamic-slice_fusion.11
  75.7 0.8 copy-done.2
  77.0 6.2 %collective-permute-done.14 = f32[2,256,256]{2,1,0:T(8,128)} collective-permute-done((f32[2,256,256]{2,1,0:T(8,128)}, f32[2,256,256]{2,1,0:T(8,128)}, u32[]{:S(2)}, u32[]{:S(2)}) %collective-permute-start.14) | collective-permute-done | bytes 524320 | tf_op jit(solution)/shard_map/ppermute | solution.py:299
  83.2 2.1 add.171
  85.8 7.5 %collective-permute-done.9 = f32[2,128,1024]{2,1,0:T(8,128)} collective-permute-done((f32[2,128,1024]{2,1,0:T(8,128)}, f32[2,128,1024]{2,1,0:T(8,128)}, u32[]{:S(2)}, u32[]{:S(2)}) %collective-permute-start.9) | collective-permute-done | bytes 1048608 | tf_op jit(solution)/shard_map/ppermute | solution.py:299
  93.4 1.7 dynamic-slice_add_fusion.2
  95.1 0.9 constant_dynamic-slice_fusion.2
  96.0 2.6 collective-permute-start.10
  98.5 1.2 constant_dynamic-slice_fusion.7
  99.8 1.5 collective-permute-start.5
  101.3 10.1 %collective-permute-done.15 = f32[2,256,256]{2,1,0:T(8,128)} collective-permute-done((f32[2,256,256]{2,1,0:T(8,128)}, f32[2,256,256]{2,1,0:T(8,128)}, u32[]{:S(2)}, u32[]{:S(2)}) %collective-permute-start.15) | collective-permute-done | bytes 524320 | tf_op jit(solution)/shard_map/ppermute | solution.py:299
  111.4 1.3 add.172
  112.7 21.8 %collective-permute-done.10 = f32[2,64,1024]{2,1,0:T(8,128)} collective-permute-done((f32[2,64,1024]{2,1,0:T(8,128)}, f32[2,64,1024]{2,1,0:T(8,128)}, u32[]{:S(2)}, u32[]{:S(2)}) %collective-permute-start.10) | collective-permute-done | bytes 524320 | tf_op jit(solution)/shard_map/ppermute | solution.py:299
  134.5 1.3 dynamic-slice_add_fusion.5
  136.1 1.7 dynamic-slice_add_fusion.1
  137.8 1.9 collective-permute-start.2
  139.7 1.6 dynamic-slice_add_fusion
  141.3 3.7 %collective-permute-done.11 = f32[2,32,1024]{2,1,0:T(8,128)S(1)} collective-permute-done((f32[2,32,1024]{2,1,0:T(8,128)S(1)}, f32[2,32,1024]{2,1,0:T(8,128)S(1)}, u32[]{:S(2)}, u32[]{:S(2)}) %collective-permute-start.11) | collective-permute-done | bytes 262176 | tf_op jit(solution)/shard_map/ppermute | solution.py:299
  145.1 1.6 collective-permute-start.12
  147.3 7.4 %collective-permute-done.12 = f32[2,16,1024]{2,1,0:T(8,128)S(1)} collective-permute-done((f32[2,16,1024]{2,1,0:T(8,128)S(1)}, f32[2,16,1024]{2,1,0:T(8,128)S(1)}, u32[]{:S(2)}, u32[]{:S(2)}) %collective-permute-start.12) | collective-permute-done | bytes 131104 | tf_op jit(solution)/shard_map/ppermute | solution.py:299
  154.7 0.9 add.173.gram_ref
  156.2 2.8 collective-permute-done.6
  159.2 0.8 collective-permute-start.7
  159.9 6.8 %collective-permute-done.3 = f32[2,32,1536]{2,1,0:T(8,128)S(1)} collective-permute-done((f32[2,32,1536]{2,1,0:T(8,128)S(1)}, f32[2,32,1536]{2,1,0:T(8,128)S(1)}, u32[]{:S(2)}, u32[]{:S(2)}) %collective-permute-start.3) | collective-permute-done | bytes 393248 | tf_op jit(solution)/shard_map/ppermute | solution.py:299
  166.8 1.7 collective-permute-start.4
  168.5 6.6 %collective-permute-done.7 = f32[2,32,1536]{2,1,0:T(8,128)S(1)} collective-permute-done((f32[2,32,1536]{2,1,0:T(8,128)S(1)}, f32[2,32,1536]{2,1,0:T(8,128)S(1)}, u32[]{:S(2)}, u32[]{:S(2)}) %collective-permute-start.7) | collective-permute-done | bytes 393248 | tf_op jit(solution)/shard_map/ppermute | solution.py:299
  175.3 6.6 %collective-permute-done.4 = f32[2,16,1536]{2,1,0:T(8,128)S(1)} collective-permute-done((f32[2,16,1536]{2,1,0:T(8,128)S(1)}, f32[2,16,1536]{2,1,0:T(8,128)S(1)}, u32[]{:S(2)}, u32[]{:S(2)}) %collective-permute-start.4) | collective-permute-done | bytes 196640 | tf_op jit(solution)/shard_map/ppermute | solution.py:299
  181.9 4.2 %collective-permute-done.8 = f32[2,16,1536]{2,1,0:T(8,128)S(1)} collective-permute-done((f32[2,16,1536]{2,1,0:T(8,128)S(1)}, f32[2,16,1536]{2,1,0:T(8,128)S(1)}, u32[]{:S(2)}, u32[]{:S(2)}) %collective-permute-start.8) | collective-permute-done | bytes 196640 | tf_op jit(solution)/shard_map/ppermute | solution.py:299
  186.1 1.5 collective-permute-start.25
  187.6 2.9 collective-permute-start.21
  191.2 1.5 collective-permute-start.26
  192.7 6.3 %collective-permute-done.17 = f32[2,16,1536]{2,1,0:T(8,128)S(1)} collective-permute-done((f32[2,16,1536]{2,1,0:T(8,128)S(1)}, f32[2,16,1536]{2,1,0:T(8,128)S(1)}, u32[]{:S(2)}, u32[]{:S(2)}) %collective-permute-start.17) | collective-permute-done | bytes 196640 | tf_op jit(solution)/shard_map/ppermute | solution.py:299
  199.0 1.7 collective-permute-start.18
  200.6 9.7 %collective-permute-done.21 = f32[2,16,1536]{2,1,0:T(8,128)S(1)} collective-permute-done((f32[2,16,1536]{2,1,0:T(8,128)S(1)}, f32[2,16,1536]{2,1,0:T(8,128)S(1)}, u32[]{:S(2)}, u32[]{:S(2)}) %collective-permute-start.21) | collective-permute-done | bytes 196640 | tf_op jit(solution)/shard_map/ppermute | solution.py:299
  210.6 3.5 collective-permute-start.27
  214.1 12.6 %collective-permute-done.22 = f32[2,32,1536]{2,1,0:T(8,128)S(1)} collective-permute-done((f32[2,32,1536]{2,1,0:T(8,128)S(1)}, f32[2,32,1536]{2,1,0:T(8,128)S(1)}, u32[]{:S(2)}, u32[]{:S(2)}) %collective-permute-start.22) | collective-permute-done | bytes 393248 | tf_op jit(solution)/shard_map/ppermute | solution.py:299
  227.2 2.3 collective-permute-done.27
  229.7 1.1 pad_maximum_fusion.2
  230.8 5.0 %collective-permute-start.28 = (f32[2,128,1024]{2,1,0:T(8,128)}, f32[2,128,1024]{2,1,0:T(8,128)}, u32[]{:S(2)}, u32[]{:S(2)}) collective-permute-start(f32[2,128,1024]{2,1,0:T(8,128)} %pad_maximum_fusion.2), channel_id=1, source_target_pairs={{0,8},{2,10},{4,12},{6,14},{8,0},{10,2},{12,4},{14,6},{16,24},{18,... | collective-permute-start | bytes 3145736 | tf_op jit(solution)/shard_map/ppermute | solution.py:299
  235.8 10.7 %collective-permute-done.19 = f32[2,64,1536]{2,1,0:T(8,128)S(1)} collective-permute-done((f32[2,64,1536]{2,1,0:T(8,128)S(1)}, f32[2,64,1536]{2,1,0:T(8,128)S(1)}, u32[]{:S(2)}, u32[]{:S(2)}) %collective-permute-start.19) | collective-permute-done | bytes 786464 | tf_op jit(solution)/shard_map/ppermute | solution.py:299
  247.7 56.9 %shard_map.96.inverse_ref = f32[2,256,256]{2,1,0:T(8,128)} custom-call(f32[2,256,256]{2,1,0:T(8,128)} %add.173.gram_ref), custom_call_target="tpu_custom_call" | custom-call | flops 50331648000 | bytes 1048576 | tf_op jit(solution)/shard_map/pallas_call | solution.py:289
  304.7 1.4 broadcast_select_fusion.5
  306.1 1.7 broadcast_select_fusion.3
  307.7 1.7 broadcast_select_fusion.1
  309.4 3.7 %maximum_maximum_fusion.cross_ref = f32[2,256,4096]{2,1,0:T(8,128)} fusion(f32[2,128,1024]{2,1,0:T(8,128)S(1)} %get-tuple-element.35, f32[2,128,1024]{2,1,0:T(8,128)S(1)} %get-tuple-element.34, f32[2,128,1536]{2,1,0:T(8,128)S(1)} %get-tuple-element.33, f32[2,128,1536]{2,1,0:T(8,128)S(1)} %get-tuple-element.32, f32[2,128,1536]{2,1,0:T(8,128)S(1)} %get-tuple-element.31, ...), kind=kLoop, calls=%fused_computation | loop fusion | flops 10485760 | bytes 16777216 | tf_op jit(solution)/shard_map/concatenate | solution.py:338
  313.1 13.1 %shard_map.97 = (f32[2,256,4096]{2,1,0:T(8,128)}, f32[2,256,1]{2,1,0:T(8,128)}) custom-call(f32[2,256,256]{2,1,0:T(8,128)} %shard_map.96.inverse_ref, f32[2,256,4096]{2,1,0:T(8,128)} %maximum_maximum_fusion.cross_ref), custom_call_target="tpu_custom_call" | custom-call | tf_op jit(solution)/shard_map/pallas_call | solution.py:151
  326.2 1.1 reduce
  327.3 3.0 psum.7.norm_ref
  330.4 25.3 %shard_map.98 = (bf16[2,512,4096]{2,1,0:T(8,128)(2,1)}, f32[2,512,2]{2,1,0:T(8,128)}, bf16[2,4096,256]{2,1,0:T(8,128)(2,1)}, bf16[2,512,4096]{2,1,0:T(8,128)(2,1)}) custom-call(f32[2,512,256]{2,1,0:T(8,128)} %add.137.power_ref, f32[2,256,256]{2,1,0:T(8,128)} %shard_map.96.inverse_ref, f32[2,1,256]{2,1,0:T(1,128)} %psum.7.norm_ref, ...), custom_call_target="tpu_custom_call" | custom-call | tf_op jit(solution)/shard_map/pallas_call | solution.py:208
  355.6 1.2 copy.15
  357.0 4.0 %pmax.7 = f32[2,512,4]{1,2,0:T(4,128)} all-reduce(f32[2,512,4]{1,2,0:T(4,128)S(1)} %select_reduce_fusion), channel_id=1, replica_groups=mesh['rows'=16,'cols'=2] {'cols'}, use_global_device_ids=true, to_apply=%region_2.3 | all-reduce | flops 4096 | bytes 32768 | tf_op jit(solution)/shard_map/pmax | solution.py:240
  (76 shorter events, 7.2 us)
Async XLA Ops:
  0.6 0.7 copy-start
  41.8 2.9 collective-permute-start
  50.3 18.3 %collective-permute-start.13 = (f32[2,256,256]{2,1,0:T(8,128)}, f32[2,256,256]{2,1,0:T(8,128)S(1)}, u32[]{:S(2)}, u32[]{:S(2)}) collective-permute-start(f32[2,256,256]{2,1,0:T(8,128)} %shard_map.95), channel_id=1, source_target_pairs={{0,2},{2,0},{4,6},{6,4},{8,10},{10,8},{12,14},{14,12},{16,18},{18,... | collective-permute-start | bytes 1572872 | tf_op jit(solution)/shard_map/ppermute | solution.py:299
  65.9 3.6 copy-start.4
  65.9 2.7 copy-start.6
  67.0 26.4 %collective-permute-start.9 = (f32[2,128,1024]{2,1,0:T(8,128)}, f32[2,128,1024]{2,1,0:T(8,128)}, u32[]{:S(2)}, u32[]{:S(2)}) collective-permute-start(f32[2,128,1024]{2,1,0:T(8,128)} %constant_dynamic-slice_fusion.3), channel_id=1, source_target_pairs={{0,8},{2,10},{4,12},{6,14},{8,0},{10,2},{12,4},{14,6},{16,24},{18,... | collective-permute-start | bytes 3145736 | tf_op jit(solution)/shard_map/ppermute | solution.py:299
  69.5 13.7 %collective-permute-start.14 = (f32[2,256,256]{2,1,0:T(8,128)}, f32[2,256,256]{2,1,0:T(8,128)}, u32[]{:S(2)}, u32[]{:S(2)}) collective-permute-start(f32[2,256,256]{2,1,0:T(8,128)} %add.170), channel_id=1, source_target_pairs={{0,4},{2,6},{4,0},{6,2},{8,12},{10,14},{12,8},{14,10},{16,20},{18,... | collective-permute-start | bytes 1572872 | tf_op jit(solution)/shard_map/ppermute | solution.py:299
  74.3 2.2 copy-start.2
  76.4 59.6 %collective-permute-start.1 = (f32[2,128,1536]{2,1,0:T(8,128)}, f32[2,128,1536]{2,1,0:T(8,128)}, u32[]{:S(2)}, u32[]{:S(2)}) collective-permute-start(f32[2,128,1536]{2,1,0:T(8,128)} %constant_dynamic-slice_fusion.11), channel_id=1, source_target_pairs={{0,2},{2,0},{4,6},{6,4},{8,10},{10,8},{12,14},{14,12},{16,18},{18,... | collective-permute-start | bytes 4718600 | tf_op jit(solution)/shard_map/ppermute | solution.py:299
  85.2 26.2 %collective-permute-start.15 = (f32[2,256,256]{2,1,0:T(8,128)}, f32[2,256,256]{2,1,0:T(8,128)}, u32[]{:S(2)}, u32[]{:S(2)}) collective-permute-start(f32[2,256,256]{2,1,0:T(8,128)} %add.171), channel_id=1, source_target_pairs={{0,8},{2,10},{4,12},{6,14},{8,0},{10,2},{12,4},{14,6},{16,24},{18,... | collective-permute-start | bytes 1572872 | tf_op jit(solution)/shard_map/ppermute | solution.py:299
  95.0 4.8 %copy-start.5 = (f32[2,128,1024]{2,1,0:T(8,128)}, f32[2,128,1024]{2,1,0:T(8,128)S(1)}, u32[]{:S(2)}) copy-start(f32[2,128,1024]{2,1,0:T(8,128)S(1)} %dynamic-slice_add_fusion.2) | copy-start | bytes 3145732
  96.0 38.5 %collective-permute-start.10 = (f32[2,64,1024]{2,1,0:T(8,128)}, f32[2,64,1024]{2,1,0:T(8,128)}, u32[]{:S(2)}, u32[]{:S(2)}) collective-permute-start(f32[2,64,1024]{2,1,0:T(8,128)} %constant_dynamic-slice_fusion.2), channel_id=1, source_target_pairs={{0,16},{2,18},{4,20},{6,22},{8,24},{10,26},{12,28},{14,30},{16,0},... | collective-permute-start | bytes 1572872 | tf_op jit(solution)/shard_map/ppermute | solution.py:299
  99.8 39.9 %collective-permute-start.5 = (f32[2,128,1536]{2,1,0:T(8,128)}, f32[2,128,1536]{2,1,0:T(8,128)}, u32[]{:S(2)}, u32[]{:S(2)}) collective-permute-start(f32[2,128,1536]{2,1,0:T(8,128)} %constant_dynamic-slice_fusion.7), channel_id=1, source_target_pairs={{0,4},{2,6},{4,0},{6,2},{8,12},{10,14},{12,8},{14,10},{16,20},{18,... | collective-permute-start | bytes 4718600 | tf_op jit(solution)/shard_map/ppermute | solution.py:299
  101.3 34.7 %copy-start.3 = (f32[2,256,1536]{2,1,0:T(8,128)S(1)}, f32[2,256,1536]{2,1,0:T(8,128)}, u32[]{:S(2)}) copy-start(f32[2,256,1536]{2,1,0:T(8,128)} %copy-done.2) | copy-start | bytes 9437188
  112.7 42.0 %collective-permute-start.16 = (f32[2,256,256]{2,1,0:T(8,128)S(1)}, f32[2,256,256]{2,1,0:T(8,128)S(1)}, u32[]{:S(2)}, u32[]{:S(2)}) collective-permute-start(f32[2,256,256]{2,1,0:T(8,128)S(1)} %add.172), channel_id=1, source_target_pairs={{0,16},{2,18},{4,20},{6,22},{8,24},{10,26},{12,28},{14,30},{16,0},... | collective-permute-start | bytes 1572872 | tf_op jit(solution)/shard_map/ppermute | solution.py:299
  135.8 9.2 %collective-permute-start.11 = (f32[2,32,1024]{2,1,0:T(8,128)S(1)}, f32[2,32,1024]{2,1,0:T(8,128)S(1)}, u32[]{:S(2)}, u32[]{:S(2)}) collective-permute-start(f32[2,32,1024]{2,1,0:T(8,128)S(1)} %constant_dynamic-slice_fusion.1), channel_id=1, source_target_pairs={{0,2},{2,0},{4,6},{6,4},{8,10},{10,8},{12,14},{14,12},{16,18},{18,... | collective-permute-start | bytes 786440 | tf_op jit(solution)/shard_map/ppermute | solution.py:299
  137.8 17.8 %collective-permute-start.2 = (f32[2,64,1536]{2,1,0:T(8,128)S(1)}, f32[2,64,1536]{2,1,0:T(8,128)S(1)}, u32[]{:S(2)}, u32[]{:S(2)}) collective-permute-start(f32[2,64,1536]{2,1,0:T(8,128)S(1)} %constant_dynamic-slice_fusion.10), channel_id=1, source_target_pairs={{0,4},{2,6},{4,0},{6,2},{8,12},{10,14},{12,8},{14,10},{16,20},{18,... | collective-permute-start | bytes 2359304 | tf_op jit(solution)/shard_map/ppermute | solution.py:299
  145.1 9.6 %collective-permute-start.12 = (f32[2,16,1024]{2,1,0:T(8,128)S(1)}, f32[2,16,1024]{2,1,0:T(8,128)S(1)}, u32[]{:S(2)}, u32[]{:S(2)}) collective-permute-start(f32[2,16,1024]{2,1,0:T(8,128)S(1)} %constant_dynamic-slice_fusion), channel_id=1, source_target_pairs={{0,4},{2,6},{4,0},{6,2},{8,12},{10,14},{12,8},{14,10},{16,20},{18,... | collective-permute-start | bytes 393224 | tf_op jit(solution)/shard_map/ppermute | solution.py:299
  146.8 12.2 %collective-permute-start.6 = (f32[2,64,1536]{2,1,0:T(8,128)S(1)}, f32[2,64,1536]{2,1,0:T(8,128)S(1)}, u32[]{:S(2)}, u32[]{:S(2)}) collective-permute-start(f32[2,64,1536]{2,1,0:T(8,128)S(1)} %constant_dynamic-slice_fusion.6), channel_id=1, source_target_pairs={{0,2},{2,0},{4,6},{6,4},{8,10},{10,8},{12,14},{14,12},{16,18},{18,... | collective-permute-start | bytes 2359304 | tf_op jit(solution)/shard_map/ppermute | solution.py:299
  155.7 11.0 %collective-permute-start.3 = (f32[2,32,1536]{2,1,0:T(8,128)S(1)}, f32[2,32,1536]{2,1,0:T(8,128)S(1)}, u32[]{:S(2)}, u32[]{:S(2)}) collective-permute-start(f32[2,32,1536]{2,1,0:T(8,128)S(1)} %constant_dynamic-slice_fusion.9), channel_id=1, source_target_pairs={{0,8},{2,10},{4,12},{6,14},{8,0},{10,2},{12,4},{14,6},{16,24},{18,... | collective-permute-start | bytes 1179656 | tf_op jit(solution)/shard_map/ppermute | solution.py:299
  159.2 15.9 %collective-permute-start.7 = (f32[2,32,1536]{2,1,0:T(8,128)S(1)}, f32[2,32,1536]{2,1,0:T(8,128)S(1)}, u32[]{:S(2)}, u32[]{:S(2)}) collective-permute-start(f32[2,32,1536]{2,1,0:T(8,128)S(1)} %constant_dynamic-slice_fusion.5), channel_id=1, source_target_pairs={{0,8},{2,10},{4,12},{6,14},{8,0},{10,2},{12,4},{14,6},{16,24},{18,... | collective-permute-start | bytes 1179656 | tf_op jit(solution)/shard_map/ppermute | solution.py:299
  166.8 15.1 %collective-permute-start.4 = (f32[2,16,1536]{2,1,0:T(8,128)S(1)}, f32[2,16,1536]{2,1,0:T(8,128)S(1)}, u32[]{:S(2)}, u32[]{:S(2)}) collective-permute-start(f32[2,16,1536]{2,1,0:T(8,128)S(1)} %constant_dynamic-slice_fusion.8), channel_id=1, source_target_pairs={{0,16},{2,18},{4,20},{6,22},{8,24},{10,26},{12,28},{14,30},{16,0},... | collective-permute-start | bytes 589832 | tf_op jit(solution)/shard_map/ppermute | solution.py:299
  175.2 10.9 %collective-permute-start.8 = (f32[2,16,1536]{2,1,0:T(8,128)S(1)}, f32[2,16,1536]{2,1,0:T(8,128)S(1)}, u32[]{:S(2)}, u32[]{:S(2)}) collective-permute-start(f32[2,16,1536]{2,1,0:T(8,128)S(1)} %constant_dynamic-slice_fusion.4), channel_id=1, source_target_pairs={{0,16},{2,18},{4,20},{6,22},{8,24},{10,26},{12,28},{14,30},{16,0},... | collective-permute-start | bytes 589832 | tf_op jit(solution)/shard_map/ppermute | solution.py:299
  186.1 5.0 %collective-permute-start.25 = (f32[2,16,1024]{2,1,0:T(8,128)S(1)}, f32[2,16,1024]{2,1,0:T(8,128)S(1)}, u32[]{:S(2)}, u32[]{:S(2)}) collective-permute-start(f32[2,16,1024]{2,1,0:T(8,128)S(1)} %dynamic-slice_add_fusion.11), channel_id=1, source_target_pairs={{0,4},{2,6},{4,0},{6,2},{8,12},{10,14},{12,8},{14,10},{16,20},{18,... | collective-permute-start | bytes 393224 | tf_op jit(solution)/shard_map/ppermute | solution.py:299
  187.6 11.3 %collective-permute-start.17 = (f32[2,16,1536]{2,1,0:T(8,128)S(1)}, f32[2,16,1536]{2,1,0:T(8,128)S(1)}, u32[]{:S(2)}, u32[]{:S(2)}) collective-permute-start(f32[2,16,1536]{2,1,0:T(8,128)S(1)} %dynamic-slice_add_fusion.10), channel_id=1, source_target_pairs={{0,16},{2,18},{4,20},{6,22},{8,24},{10,26},{12,28},{14,30},{16,0},... | collective-permute-start | bytes 589832 | tf_op jit(solution)/shard_map/ppermute | solution.py:299
  187.6 22.8 %collective-permute-start.21 = (f32[2,16,1536]{2,1,0:T(8,128)S(1)}, f32[2,16,1536]{2,1,0:T(8,128)S(1)}, u32[]{:S(2)}, u32[]{:S(2)}) collective-permute-start(f32[2,16,1536]{2,1,0:T(8,128)S(1)} %dynamic-slice_add_fusion.9), channel_id=1, source_target_pairs={{0,16},{2,18},{4,20},{6,22},{8,24},{10,26},{12,28},{14,30},{16,0},... | collective-permute-start | bytes 589832 | tf_op jit(solution)/shard_map/ppermute | solution.py:299
  191.2 19.3 %collective-permute-start.26 = (f32[2,32,1024]{2,1,0:T(8,128)S(1)}, f32[2,32,1024]{2,1,0:T(8,128)S(1)}, u32[]{:S(2)}, u32[]{:S(2)}) collective-permute-start(f32[2,32,1024]{2,1,0:T(8,128)S(1)} %pad_maximum_fusion.8), channel_id=1, source_target_pairs={{0,2},{2,0},{4,6},{6,4},{8,10},{10,8},{12,14},{14,12},{16,18},{18,... | collective-permute-start | bytes 786440 | tf_op jit(solution)/shard_map/ppermute | solution.py:299
  199.0 15.2 %collective-permute-start.18 = (f32[2,32,1536]{2,1,0:T(8,128)S(1)}, f32[2,32,1536]{2,1,0:T(8,128)S(1)}, u32[]{:S(2)}, u32[]{:S(2)}) collective-permute-start(f32[2,32,1536]{2,1,0:T(8,128)S(1)} %pad_maximum_fusion.6), channel_id=1, source_target_pairs={{0,8},{2,10},{4,12},{6,14},{8,0},{10,2},{12,4},{14,6},{16,24},{18,... | collective-permute-start | bytes 1179656 | tf_op jit(solution)/shard_map/ppermute | solution.py:299
  210.4 16.3 %collective-permute-start.22 = (f32[2,32,1536]{2,1,0:T(8,128)S(1)}, f32[2,32,1536]{2,1,0:T(8,128)S(1)}, u32[]{:S(2)}, u32[]{:S(2)}) collective-permute-start(f32[2,32,1536]{2,1,0:T(8,128)S(1)} %pad_maximum_fusion.7), channel_id=1, source_target_pairs={{0,8},{2,10},{4,12},{6,14},{8,0},{10,2},{12,4},{14,6},{16,24},{18,... | collective-permute-start | bytes 1179656 | tf_op jit(solution)/shard_map/ppermute | solution.py:299
  210.6 18.9 %collective-permute-start.27 = (f32[2,64,1024]{2,1,0:T(8,128)S(1)}, f32[2,64,1024]{2,1,0:T(8,128)S(1)}, u32[]{:S(2)}, u32[]{:S(2)}) collective-permute-start(f32[2,64,1024]{2,1,0:T(8,128)S(1)} %pad_maximum_fusion.5), channel_id=1, source_target_pairs={{0,16},{2,18},{4,20},{6,22},{8,24},{10,26},{12,28},{14,30},{16,0},... | collective-permute-start | bytes 1572872 | tf_op jit(solution)/shard_map/ppermute | solution.py:299
  226.9 19.6 %collective-permute-start.19 = (f32[2,64,1536]{2,1,0:T(8,128)S(1)}, f32[2,64,1536]{2,1,0:T(8,128)S(1)}, u32[]{:S(2)}, u32[]{:S(2)}) collective-permute-start(f32[2,64,1536]{2,1,0:T(8,128)S(1)} %pad_maximum_fusion.3), channel_id=1, source_target_pairs={{0,4},{2,6},{4,0},{6,2},{8,12},{10,14},{12,8},{14,10},{16,20},{18,... | collective-permute-start | bytes 2359304 | tf_op jit(solution)/shard_map/ppermute | solution.py:299
  227.1 20.2 %collective-permute-start.23 = (f32[2,64,1536]{2,1,0:T(8,128)S(1)}, f32[2,64,1536]{2,1,0:T(8,128)S(1)}, u32[]{:S(2)}, u32[]{:S(2)}) collective-permute-start(f32[2,64,1536]{2,1,0:T(8,128)S(1)} %pad_maximum_fusion.4), channel_id=1, source_target_pairs={{0,2},{2,0},{4,6},{6,4},{8,10},{10,8},{12,14},{14,12},{16,18},{18,... | collective-permute-start | bytes 2359304 | tf_op jit(solution)/shard_map/ppermute | solution.py:299
  230.8 73.9 %collective-permute-start.28 = (f32[2,128,1024]{2,1,0:T(8,128)}, f32[2,128,1024]{2,1,0:T(8,128)}, u32[]{:S(2)}, u32[]{:S(2)}) collective-permute-start(f32[2,128,1024]{2,1,0:T(8,128)} %pad_maximum_fusion.2), channel_id=1, source_target_pairs={{0,8},{2,10},{4,12},{6,14},{8,0},{10,2},{12,4},{14,6},{16,24},{18,... | collective-permute-start | bytes 3145736 | tf_op jit(solution)/shard_map/ppermute | solution.py:299
  246.8 59.2 %collective-permute-start.20 = (f32[2,128,1536]{2,1,0:T(8,128)S(1)}, f32[2,128,1536]{2,1,0:T(8,128)}, u32[]{:S(2)}, u32[]{:S(2)}) collective-permute-start(f32[2,128,1536]{2,1,0:T(8,128)S(1)} %pad_maximum_fusion), channel_id=1, source_target_pairs={{0,2},{2,0},{4,6},{6,4},{8,10},{10,8},{12,14},{14,12},{16,18},{18,... | collective-permute-start | bytes 4718600 | tf_op jit(solution)/shard_map/ppermute | solution.py:299
  247.6 60.1 %collective-permute-start.24 = (f32[2,128,1536]{2,1,0:T(8,128)S(1)}, f32[2,128,1536]{2,1,0:T(8,128)}, u32[]{:S(2)}, u32[]{:S(2)}) collective-permute-start(f32[2,128,1536]{2,1,0:T(8,128)S(1)} %pad_maximum_fusion.1), channel_id=1, source_target_pairs={{0,4},{2,6},{4,0},{6,2},{8,12},{10,14},{12,8},{14,10},{16,20},{18,... | collective-permute-start | bytes 4718600 | tf_op jit(solution)/shard_map/ppermute | solution.py:299
  330.4 30.6 %copy-start.1 = (f32[2,512,4]{1,2,0:T(4,128)S(1)}, f32[2,512,4]{1,2,0:T(4,128)}, u32[]{:S(2)}) copy-start(f32[2,512,4]{1,2,0:T(4,128)} %param.7) | copy-start | bytes 49156
